TPU v7x, 32 devices: a whole 2x2x4 slice. The times are simulated.
32 devices in a mesh: dp: 8 (over z, x), tensor: 4 (over y, core).
Axes of the slice: x: 2, y: 2, z: 4, core: 2. Of those that a mesh axis runs over, the one named last changes fastest.
Arguments:
- inputs: bfloat16 [8192, 768], P('dp'), may hold values from -6 to 6
- lengths: int32 [8], P('dp'), may hold values from 32 to 1024, as said below
- qkv_weight: bfloat16 [2, 768, 3, 768], P(None, None, None, 'tensor'), may hold values from -0.21875 to 0.21875
- out_weight: bfloat16 [2, 768, 768], P(None, 'tensor'), may hold values from -0.875 to 0.875
- up_weight: bfloat16 [2, 768, 3072], P(None, None, 'tensor'), may hold values from -0.21875 to 0.21875
- down_weight: bfloat16 [2, 3072, 768], P(None, 'tensor'), may hold values from -0.15625 to 0.15625
- norm_gain: float32 [2, 2, 768], replicated, may hold values from 0.5 to 1.5
- norm_bias: float32 [2, 2, 768], replicated, may hold values from -1.5 to 1.5
- cotangent: bfloat16 [8192, 768], P('dp'), may hold values from -6 to 6
Outputs:
- activations: bfloat16 [8192, 768], P('dp')
- input_grad: float32 [8192, 768], P('dp')
- grad_qkv: float32 [2, 768, 3, 768], P(None, None, None, 'tensor')
- grad_out: float32 [2, 768, 768], P(None, 'tensor')
- grad_up: float32 [2, 768, 3072], P(None, None, 'tensor')
- grad_down: float32 [2, 3072, 768], P(None, 'tensor')
- grad_gain: float32 [2, 2, 768], replicated
- grad_bias: float32 [2, 2, 768], replicated
Inputs may be any that keep to these rules, and one draw needn't show every extreme that they name: `lengths`: slots from a sequence's length on are padding; in every draw some sequence uses all 1024 slots.
All inputs are finite; a program needn't handle non-finite values.
Results may differ from a plain program's by a relative error of at most 0.035.
Values may be sent and summed in bfloat16 or wider, within the bound.
A program may use at most 128 MiB of HBM per device.

v0:
```python
import jax
import jax.numpy as jnp
from jax import lax
from jax.sharding import PartitionSpec as P

HEAD_DIM = 64


def norm_rows(values_in, gain_row, bias_row):
    centre = values_in - jnp.mean(values_in, axis=-1, keepdims=True)
    spread = jnp.mean(centre * centre, axis=-1, keepdims=True)
    return centre * lax.rsqrt(spread + 1e-05) * gain_row + bias_row


def exact_gelu(values_in):
    return jax.nn.gelu(values_in, approximate=False)


def allowed_block(row_start, block_rows, seq_len, length_one):
    query_pos = row_start + jnp.arange(block_rows, dtype=jnp.int32)[:, None]
    key_pos = jnp.arange(seq_len, dtype=jnp.int32)[None, :]
    return (key_pos <= query_pos) & (key_pos < length_one)


def block_inputs(queries, key_rows, value_rows, lengths, block_id, per_seq, block_rows):
    seq_id = block_id // per_seq
    row_start = block_id % per_seq * block_rows
    query_seq = lax.dynamic_index_in_dim(queries, seq_id, 0, False)
    query_block = lax.dynamic_slice_in_dim(query_seq, row_start, block_rows, 0)
    keys_seq = lax.dynamic_index_in_dim(key_rows, seq_id, 0, False)
    values_seq = lax.dynamic_index_in_dim(value_rows, seq_id, 0, False)
    length_one = lax.dynamic_index_in_dim(lengths, seq_id, 0, False)
    return (seq_id, row_start, query_block, keys_seq, values_seq, length_one)


def attend_forward(queries, key_rows, value_rows, lengths, factor):
    seq_count, seq_len = (queries.shape[0], queries.shape[1])
    block_rows = min(512, seq_len)
    per_seq = seq_len // block_rows

    def one_block(block_id):
        seq_id, row_start, query_block, keys_seq, values_seq, length_one = block_inputs(
            queries, key_rows, value_rows, lengths, block_id, per_seq, block_rows
        )
        scores = (
            jnp.einsum("qhe,khe->hqk", query_block, keys_seq, preferred_element_type=jnp.float32)
            * factor
        )
        scores = jnp.where(
            allowed_block(row_start, block_rows, seq_len, length_one)[None], scores, -1e30
        )
        maximum = jnp.max(scores, axis=-1, keepdims=True)
        exponent = jnp.exp(scores - maximum)
        summed = jnp.sum(exponent, axis=-1, keepdims=True)
        softmax_low = (exponent / summed).astype(jnp.bfloat16)
        context = jnp.einsum(
            "hqk,khe->qhe", softmax_low, values_seq, preferred_element_type=jnp.float32
        )
        return (context.astype(jnp.bfloat16), (maximum + jnp.log(summed))[..., 0])

    context, log_total = lax.map(one_block, jnp.arange(seq_count * per_seq, dtype=jnp.int32))
    return (context.reshape(seq_count * seq_len, -1), log_total)


def attend_backward(queries, key_rows, value_rows, lengths, log_total, context_grad, factor):
    seq_count, seq_len = (queries.shape[0], queries.shape[1])
    block_rows = min(512, seq_len)
    per_seq = seq_len // block_rows
    zeros_acc = jnp.zeros(key_rows.shape, jnp.float32)

    def one_block(accumulated, block_id):
        key_acc, value_acc = accumulated
        seq_id, row_start, query_block, keys_seq, values_seq, length_one = block_inputs(
            queries, key_rows, value_rows, lengths, block_id, per_seq, block_rows
        )
        grad_block = lax.dynamic_slice_in_dim(
            lax.dynamic_index_in_dim(context_grad, seq_id, 0, False), row_start, block_rows, 0
        )
        scores = (
            jnp.einsum("qhe,khe->hqk", query_block, keys_seq, preferred_element_type=jnp.float32)
            * factor
        )
        scores = jnp.where(
            allowed_block(row_start, block_rows, seq_len, length_one)[None], scores, -1e30
        )
        softmax_rows = jnp.exp(
            scores - lax.dynamic_index_in_dim(log_total, block_id, 0, False)[:, :, None]
        )
        softmax_low = softmax_rows.astype(jnp.bfloat16)
        prob_grad = jnp.einsum(
            "qhe,khe->hqk", grad_block, values_seq, preferred_element_type=jnp.float32
        )
        inner_sum = jnp.sum(softmax_rows * prob_grad, axis=-1, keepdims=True)
        score_grad = (softmax_rows * (prob_grad - inner_sum)).astype(jnp.bfloat16)
        query_grad = (
            jnp.einsum("hqk,khe->qhe", score_grad, keys_seq, preferred_element_type=jnp.float32)
            * factor
        )
        key_part = (
            jnp.einsum("hqk,qhe->khe", score_grad, query_block, preferred_element_type=jnp.float32)
            * factor
        )
        value_part = jnp.einsum(
            "hqk,qhe->khe", softmax_low, grad_block, preferred_element_type=jnp.float32
        )
        key_acc = lax.dynamic_update_index_in_dim(
            key_acc, lax.dynamic_index_in_dim(key_acc, seq_id, 0, False) + key_part, seq_id, 0
        )
        value_acc = lax.dynamic_update_index_in_dim(
            value_acc, lax.dynamic_index_in_dim(value_acc, seq_id, 0, False) + value_part, seq_id, 0
        )
        return ((key_acc, value_acc), query_grad)

    (key_acc, value_acc), query_grad = lax.scan(
        one_block, (zeros_acc, zeros_acc), jnp.arange(seq_count * per_seq, dtype=jnp.int32)
    )
    return (query_grad.reshape(queries.shape), key_acc, value_acc)


def per_device(
    inputs, lengths, qkv_weight, out_weight, up_weight, down_weight, norm_gain, norm_bias, cotangent
):
    layer_total = qkv_weight.shape[0]
    row_total, width_all = inputs.shape
    seq_count = lengths.shape[0]
    seq_len = row_total // seq_count
    part_width = qkv_weight.shape[3]
    head_count = part_width // HEAD_DIM
    factor = HEAD_DIM ** (-0.5)
    positions = jnp.arange(seq_len, dtype=jnp.int32)
    valid_rows = (positions[None, :] < lengths[:, None]).astype(jnp.float32).reshape(row_total, 1)

    def group_total(partial_value):
        return lax.psum(partial_value.astype(jnp.bfloat16), "tensor").astype(jnp.float32)

    def layer_weights(layer_id):
        return (
            qkv_weight[layer_id].reshape(width_all, -1),
            out_weight[layer_id],
            up_weight[layer_id],
            down_weight[layer_id],
            norm_gain[layer_id],
            norm_bias[layer_id],
        )

    stream = inputs.astype(jnp.float32)
    stored = []
    for layer_id in range(layer_total):
        proj_qkv, proj_out, proj_up, proj_down, gain_rows, biases = layer_weights(layer_id)
        normed = norm_rows(stream, gain_rows[0], biases[0]).astype(jnp.bfloat16)
        projected = jnp.dot(normed, proj_qkv, preferred_element_type=jnp.float32).astype(
            jnp.bfloat16
        )
        projected = projected.reshape(seq_count, seq_len, 3, head_count, HEAD_DIM)
        queries, key_rows, value_rows = (projected[:, :, 0], projected[:, :, 1], projected[:, :, 2])
        context, log_total = attend_forward(queries, key_rows, value_rows, lengths, factor)
        middle = stream + group_total(
            jnp.dot(context, proj_out, preferred_element_type=jnp.float32)
        )
        normed_mid = norm_rows(middle, gain_rows[1], biases[1]).astype(jnp.bfloat16)
        hidden = jnp.dot(normed_mid, proj_up, preferred_element_type=jnp.float32)
        activated = exact_gelu(hidden).astype(jnp.bfloat16)
        stored.append(
            (stream, middle, normed, normed_mid, queries, key_rows, value_rows, context, log_total)
        )
        stream = valid_rows * (
            middle + group_total(jnp.dot(activated, proj_down, preferred_element_type=jnp.float32))
        )
    outputs = stream.astype(jnp.bfloat16)
    upstream = cotangent.astype(jnp.float32)
    grad_layers = []
    for layer_id in reversed(range(layer_total)):
        proj_qkv, proj_out, proj_up, proj_down, gain_rows, biases = layer_weights(layer_id)
        stream_in, middle, normed, normed_mid, queries, key_rows, value_rows, context, log_total = (
            stored[layer_id]
        )
        upstream = valid_rows * upstream
        down_grad = upstream.astype(jnp.bfloat16)
        hidden = jnp.dot(normed_mid, proj_up, preferred_element_type=jnp.float32)
        activated, gelu_pull = jax.vjp(exact_gelu, hidden)
        grad_down = jnp.einsum(
            "tf,td->fd",
            activated.astype(jnp.bfloat16),
            down_grad,
            preferred_element_type=jnp.float32,
        )
        act_grad = jnp.einsum("td,fd->tf", down_grad, proj_down, preferred_element_type=jnp.float32)
        hidden_grad = gelu_pull(act_grad)[0].astype(jnp.bfloat16)
        grad_up = jnp.einsum(
            "td,tf->df", normed_mid, hidden_grad, preferred_element_type=jnp.float32
        )
        mid_norm_grad = group_total(
            jnp.einsum("tf,df->td", hidden_grad, proj_up, preferred_element_type=jnp.float32)
        )
        unused_mid, norm_pull = jax.vjp(norm_rows, middle, gain_rows[1], biases[1])
        middle_grad, gain_mid, bias_mid = norm_pull(mid_norm_grad)
        upstream = upstream + middle_grad
        out_grad = upstream.astype(jnp.bfloat16)
        grad_out = jnp.einsum("te,td->ed", context, out_grad, preferred_element_type=jnp.float32)
        context_grad = jnp.einsum(
            "td,ed->te", out_grad, proj_out, preferred_element_type=jnp.float32
        ).astype(jnp.bfloat16)
        context_grad = context_grad.reshape(seq_count, seq_len, head_count, HEAD_DIM)
        query_grad, key_grad, value_grad = attend_backward(
            queries, key_rows, value_rows, lengths, log_total, context_grad, factor
        )
        proj_grad = (
            jnp.stack((query_grad, key_grad, value_grad), axis=2)
            .astype(jnp.bfloat16)
            .reshape(row_total, -1)
        )
        grad_qkv = jnp.einsum(
            "td,tc->dc", normed, proj_grad, preferred_element_type=jnp.float32
        ).reshape(width_all, 3, part_width)
        in_norm_grad = group_total(
            jnp.einsum("tc,dc->td", proj_grad, proj_qkv, preferred_element_type=jnp.float32)
        )
        unused_in, norm_pull = jax.vjp(norm_rows, stream_in, gain_rows[0], biases[0])
        stream_grad, gain_in, bias_in = norm_pull(in_norm_grad)
        upstream = upstream + stream_grad
        grad_layers.append(
            (
                grad_qkv,
                grad_out,
                grad_up,
                grad_down,
                jnp.stack((gain_in, gain_mid)),
                jnp.stack((bias_in, bias_mid)),
            )
        )
    grad_layers = grad_layers[::-1]
    stacked = tuple((jnp.stack([entry[member] for entry in grad_layers]) for member in range(6)))
    totals = (
        lax.psum(stacked[0].astype(jnp.bfloat16), "dp").astype(jnp.float32),
        lax.psum(stacked[1].astype(jnp.bfloat16), "dp").astype(jnp.float32),
        lax.psum(stacked[2].astype(jnp.bfloat16), "dp").astype(jnp.float32),
        lax.psum(stacked[3].astype(jnp.bfloat16), "dp").astype(jnp.float32),
        lax.psum(stacked[4].astype(jnp.bfloat16), "dp").astype(jnp.float32),
        lax.psum(stacked[5].astype(jnp.bfloat16), "dp").astype(jnp.float32),
    )
    return (outputs, upstream, totals[0], totals[1], totals[2], totals[3], totals[4], totals[5])


def solution(mesh):
    in_specs = (
        P("dp", None),
        P("dp"),
        P(None, None, None, "tensor"),
        P(None, "tensor", None),
        P(None, None, "tensor"),
        P(None, "tensor", None),
        P(),
        P(),
        P("dp", None),
    )
    out_specs = (
        P("dp", None),
        P("dp", None),
        P(None, None, None, "tensor"),
        P(None, "tensor", None),
        P(None, None, "tensor"),
        P(None, "tensor", None),
        P(),
        P(),
    )
    return jax.shard_map(
        per_device, mesh=mesh, in_specs=in_specs, out_specs=out_specs, check_vma=False
    )
```

profile of v0, /device:TPU:0, one launch (start us, length us, event | category | flops | bytes accessed | tf_op | source)
XLA Modules:
  0.0 847.1 jit_solution(10513101290034813167)
XLA Ops:
  9.1 2.0 fusion.125
  15.8 20.2 %while.60 = (s32[]{:T(128)}, bf16[2,512,3,64]{1,3,2,0:T(8,128)(2,1)S(1)}, f32[2,3,512]{2,1,0:T(4,128)S(1)}, s32[2]{0:T(128)S(1)}, s32[1]{0:T(128)}, /*index=5*/b...) while((s32[]{:T(128)}, ...), condition=%wide.region_5.6_spmd, body=%wide.region_2.5_spmd.sunk | while | flops 422674432 | bytes 22217024 | solution.py:61
  22.7 3.2 fusion.289
  32.8 3.2 fusion.289
  39.7 45.1 %all-reduce.12.cloned.1.call-done = bf16[1024,768]{1,0:T(8,128)(2,1)} async-done(((bf16[1024,768]{1,0:T(8,128)(2,1)}), bf16[1024,768]{1,0:T(8,128)(2,1)}) %all-reduce.12.cloned.1.call-update) | async-done | bytes 1572880 | tf_op jit(solution)/shard_map/psum | solution.py:134
  84.8 2.0 fusion.141
  89.3 9.0 %multiply_convert_fusion.4 = (bf16[1024,768]{1,0:T(8,128)(2,1)S(1)}, f32[1024,768]{1,0:T(8,128)}, f32[1024,768]{1,0:T(8,128)}) fusion(bf16[1024,768]{1,0:T(8,128)(2,1)S(1)} %add_convert_fusion.4, bf16[2,768,768]{2,1,0:T(8,128)(2,1)S(1)} %copy-done.112), kind=kOutput, calls=%fused_computation.192 | convolution fusion | flops 1259077632 | bytes 10616832 | tf_op jit(solution)/shard_map/dot_general | solution.py:161
  99.5 2.5 convolution_convert_fusion.6
  102.9 42.2 %all-reduce.14.cloned.1.call-done = bf16[1024,768]{1,0:T(8,128)(2,1)} async-done(((bf16[1024,768]{1,0:T(8,128)(2,1)}), bf16[1024,768]{1,0:T(8,128)(2,1)}) %all-reduce.14.cloned.1.call-update) | async-done | bytes 1572880 | tf_op jit(solution)/shard_map/psum | solution.py:134
  145.1 2.2 fusion.216
  150.7 18.1 %while.61 = (s32[]{:T(128)}, bf16[2,512,3,64]{1,3,2,0:T(8,128)(2,1)S(1)}, f32[2,3,512]{2,1,0:T(4,128)S(1)}, s32[2]{0:T(128)S(1)}, s32[1]{0:T(128)}, /*index=5*/b...) while((s32[]{:T(128)}, ...), condition=%wide.region_15.16_spmd, body=%wide.region_12.15_spmd.sunk | while | flops 422674432 | bytes 22217024 | solution.py:61
  157.6 2.2 fusion.294
  166.6 2.2 fusion.294
  172.2 42.8 %all-reduce.16.cloned.1.call-done = bf16[1024,768]{1,0:T(8,128)(2,1)} async-done(((bf16[1024,768]{1,0:T(8,128)(2,1)}), bf16[1024,768]{1,0:T(8,128)(2,1)}) %all-reduce.16.cloned.1.call-update) | async-done | bytes 1572880 | tf_op jit(solution)/shard_map/psum | solution.py:134
  215.0 2.7 fusion.215
  220.5 18.1 %multiply_convert_fusion.3 = (bf16[1024,768]{1,0:T(8,128)(2,1)}, f32[1024,768]{1,0:T(8,128)S(1)}, f32[1024,768]{1,0:T(8,128)S(1)}) fusion(bf16[1024,768]{1,0:T(8,128)(2,1)S(1)} %add_convert_fusion.2, bf16[2,768,768]{2,1,0:T(8,128)(2,1)S(1)} %copy-done.113), kind=kOutput, calls=%fused_computation.173 | convolution fusion | flops 1259077632 | bytes 10616832 | tf_op jit(solution)/shard_map/dot_general | solution.py:161
  238.7 2.4 add_convert_fusion.1
  242.2 2.6 convolution_convert_fusion.3
  244.9 4.4 fusion.155
  249.3 38.7 %all-reduce.18.cloned.1.call-done = bf16[1024,768]{1,0:T(8,128)(2,1)} async-done(((bf16[1024,768]{1,0:T(8,128)(2,1)}), bf16[1024,768]{1,0:T(8,128)(2,1)}) %all-reduce.18.cloned.1.call-update) | async-done | bytes 1572880 | tf_op jit(solution)/shard_map/psum | solution.py:134
  288.0 3.4 fusion.121
  297.2 45.2 %while.62 = (s32[]{:T(128)}, f32[1,1024,3,64]{1,3,2,0:T(8,128)S(1)}, f32[1,1024,3,64]{1,3,2,0:T(8,128)S(1)}, bf16[2,512,3,64]{1,0,3,2:T(2,128)(2,1)}, s32[2]{0:T...) while((s32[]{:T(128)}, ...), condition=%wide.region_25.26_spmd, body=%wide.region_23.25_spmd.sunk | while | flops 1032060928 | bytes 55431548 | solution.py:114
  303.8 1.9 fusion.306
  305.7 2.5 multiply_reduce_fusion.7
  312.3 7.6 dynamic_update_slice.58
  326.4 2.0 fusion.306
  328.3 2.5 multiply_reduce_fusion.7
  334.8 7.6 dynamic_update_slice.58
  344.8 2.6 convolution_convert_fusion.1
  347.7 4.4 convolution_convert_fusion.4
  352.2 2.6 fusion.157
  356.1 34.5 %all-reduce.20.cloned.1.call-done = bf16[1024,768]{1,0:T(8,128)(2,1)} async-done(((bf16[1024,768]{1,0:T(8,128)(2,1)}), bf16[1024,768]{1,0:T(8,128)(2,1)}) %all-reduce.20.cloned.1.call-update) | async-done | bytes 1572880 | tf_op jit(solution)/shard_map/psum | solution.py:134
  390.6 2.3 fusion.119
  392.9 2.5 fusion.122
  395.4 1.9 add_multiply_fusion
  398.0 2.1 copy-done.116
  400.1 2.2 add_convert_fusion
  403.4 2.6 convolution_convert_fusion.2
  406.1 3.7 fusion.158
  409.9 2.5 fusion.156
  412.4 36.7 %all-reduce.22.cloned.1.call-done = bf16[1024,768]{1,0:T(8,128)(2,1)} async-done(((bf16[1024,768]{1,0:T(8,128)(2,1)}), bf16[1024,768]{1,0:T(8,128)(2,1)}) %all-reduce.22.cloned.1.call-update) | async-done | bytes 1572880 | tf_op jit(solution)/shard_map/psum | solution.py:134
  449.1 2.6 fusion.118
  451.7 3.0 fusion.123
  460.4 51.8 %while.63 = (s32[]{:T(128)}, f32[1,1024,3,64]{1,3,2,0:T(8,128)S(1)}, f32[1,1024,3,64]{1,3,2,0:T(8,128)}, bf16[2,512,3,64]{1,0,3,2:T(2,128)(2,1)}, s32[2]{0:T(128...) while((s32[]{:T(128)}, ...), condition=%wide.region_34.35_spmd, body=%wide.region_32.34_spmd.sunk | while | flops 1032060928 | bytes 55427452 | solution.py:114
  467.0 4.0 fusion.319
  471.1 3.6 multiply_reduce_fusion.8
  478.6 7.6 dynamic_update_slice.59
  492.8 4.0 fusion.319
  496.8 3.6 multiply_reduce_fusion.8
  504.4 7.6 dynamic_update_slice.59
  516.0 2.6 convolution_convert_fusion
  518.6 3.4 pad_maximum_fusion.1
  530.8 1.8 reduce.3
  534.8 52.6 %all-reduce.26.cloned.1.call-done = (bf16[1024,768]{1,0:T(8,128)(2,1)}, bf16[1024,768]{1,0:T(8,128)(2,1)}) async-done(((bf16[1024,768]{1,0:T(8,128)(2,1)}, bf16[1024,768]{1,0:T(8,128)(2,1)}), (bf16[1024,768]{1,0:T(8,128)(2,1)}, bf16[1024,768]{1,0:T(8,128)(2,1)})) %all-reduce.26.cloned.1.call-update) | async-done | bytes 3145744 | tf_op jit(solution)/shard_map/psum | solution.py:134
  589.2 2.3 fusion.126
  591.5 1.9 fusion.124
  593.6 39.3 %all-reduce = (bf16[2,2,768]{2,1,0:T(2,128)(2,1)S(1)}, bf16[2,2,768]{2,1,0:T(2,128)(2,1)S(1)}) all-reduce(bf16[2,2,768]{2,1,0:T(2,128)(2,1)S(1)} %pad_maximum_fusion.4, bf16[2,2,768]{2,1,0:T(2,128)(2,1)S(1)} %pad_maximum_fusion.5), channel_id=1, replica_groups=mesh['dp'=8,'tensor'=4] {'dp'}, use_global_device_ids=true, to_apply=%region_46.47 | all-reduce | flops 6144 | bytes 24576 | tf_op jit(solution)/shard_map/psum | solution.py:238
  634.1 4.3 multiply_convert_fusion.2
  638.4 2.4 add_add_fusion.4
  640.8 188.1 %all-reduce.24.cloned.1.call-done = (bf16[2,768,3,192]{1,3,2,0:T(8,128)(2,1)}, bf16[2,192,768]{2,1,0:T(8,128)(2,1)}, bf16[2,768,768]{2,1,0:T(8,128)(2,1)}, bf16[2,768,768]{2,1,0:T(8,128)(2,1)}) async-done(((bf16[2,768,3,192]{1,3,2,0:T(8,128)(2,1)}, bf16[2,192,768]{2,1,0:T(8,128)(2,1)}, bf16[2,768,768]{2,1,0:T(8,128)(2,1)}, bf16[2,768,768]{2,1,0:T(8,128)(2,1)}), (bf16[2,768,3,192]{1,3,2,0:T(8,128)(2,1)}, ...) | async-done | bytes 7077904 | tf_op jit(solution)/shard_map/psum | solution.py:234
  828.9 2.3 convert_element_type.279
  831.2 3.6 convert_element_type.278
  834.8 2.5 convert_element_type.280
  837.3 2.5 convert_element_type.281
  (413 shorter events, 108.1 us)
Async XLA Ops:
  7.2 4.5 copy-start.40
  7.2 77.6 %all-reduce.12.cloned.1.call-start = ((), (), s32[]{:S(2)}) async-start(), calls=%async_computation | async-start | bytes 3145728 | tf_op jit(solution)/shard_map/psum | solution.py:134
  7.2 5.5 copy-start.100
  7.2 5.5 copy-start.101
  7.2 6.3 copy-start
  9.1 5.8 copy-start.73
  13.5 74.1 %copy-start.62 = (f32[768]{0:T(1024)}, f32[768]{0:T(1024)S(1)}, u32[]{:S(2)}) copy-start(f32[768]{0:T(1024)S(1)} %get-tuple-element.634) | copy-start | bytes 9220
  13.5 134.9 %copy-start.77 = (f32[768]{0:T(1024)}, f32[768]{0:T(1024)S(1)}, u32[]{:S(2)}) copy-start(f32[768]{0:T(1024)S(1)} %get-tuple-element.632) | copy-start | bytes 9220
  13.5 134.9 %copy-start.107 = (f32[768]{0:T(1024)}, f32[768]{0:T(1024)S(1)}, u32[]{:S(2)}) copy-start(f32[768]{0:T(1024)S(1)} %get-tuple-element.519) | copy-start | bytes 9220
  15.8 21.5 %copy-start.44 = (bf16[2,192,768]{2,1,0:T(8,128)(2,1)S(1)}, bf16[2,192,768]{2,1,0:T(8,128)(2,1)}, u32[]{:S(2)}) copy-start(bf16[2,192,768]{2,1,0:T(8,128)(2,1)} %param.20) | copy-start | bytes 1769476
  36.0 3.7 copy-start.12
  36.0 3.7 copy-start.58
  36.0 50.8 %copy-start.5 = (bf16[1,1024,3,64]{1,3,2,0:T(8,128)(2,1)}, bf16[1,1024,3,64]{1,3,2,0:T(8,128)(2,1)S(1)}, u32[]{:S(2)}) copy-start(bf16[1,1024,3,64]{1,3,2,0:T(8,128)(2,1)S(1)} %get-tuple-element.1076) | copy-start | bytes 1179652
  39.1 106.0 %all-reduce.14.cloned.1.call-start = ((), (), s32[]{:S(2)}) async-start(), calls=%async_computation.1 | async-start | bytes 3145728 | tf_op jit(solution)/shard_map/psum | solution.py:134
  87.6 10.7 %copy-start.93 = (f32[1024]{0:T(1024)}, f32[1024]{0:T(1024)S(1)}, u32[]{:S(2)}) copy-start(f32[1024]{0:T(1024)S(1)} %multiply_reduce_fusion.4) | copy-start | bytes 12292
  87.6 10.7 %copy-start.75 = (f32[1024]{0:T(1024)}, f32[1024]{0:T(1024)S(1)}, u32[]{:S(2)}) copy-start(f32[1024]{0:T(1024)S(1)} %fusion.206) | copy-start | bytes 12292
  89.3 9.0 %copy-start.41 = (bf16[1024,768]{1,0:T(8,128)(2,1)}, bf16[1024,768]{1,0:T(8,128)(2,1)S(1)}, u32[]{:S(2)}) copy-start(bf16[1024,768]{1,0:T(8,128)(2,1)S(1)} %add_convert_fusion.4) | copy-start | bytes 4718596
  89.3 10.2 %copy-start.109 = (bf16[2,768,768]{2,1,0:T(8,128)(2,1)S(1)}, bf16[2,768,768]{2,1,0:T(8,128)(2,1)}, u32[]{:S(2)}) copy-start(bf16[2,768,768]{2,1,0:T(8,128)(2,1)} %param.22) | copy-start | bytes 7077892
  102.0 112.9 %all-reduce.16.cloned.1.call-start = ((), (), s32[]{:S(2)}) async-start(), calls=%async_computation.2 | async-start | bytes 3145728 | tf_op jit(solution)/shard_map/psum | solution.py:134
  102.9 44.4 %copy-start.64 = (f32[1024]{0:T(1024)}, f32[1024]{0:T(1024)S(1)}, u32[]{:S(2)}) copy-start(f32[1024]{0:T(1024)S(1)} %fusion.204) | copy-start | bytes 12292
  150.7 19.4 %copy-start.45 = (bf16[2,192,768]{2,1,0:T(8,128)(2,1)S(1)}, bf16[2,192,768]{2,1,0:T(8,128)(2,1)}, u32[]{:S(2)}) copy-start(bf16[2,192,768]{2,1,0:T(8,128)(2,1)} %param.20) | copy-start | bytes 1769476
  171.9 116.0 %all-reduce.18.cloned.1.call-start = ((), (), s32[]{:S(2)}) async-start(), calls=%async_computation.3 | async-start | bytes 3145728 | tf_op jit(solution)/shard_map/psum | solution.py:134
  217.7 73.6 %copy-start.2 = (f32[1024,768]{1,0:T(8,128)}, f32[1024,768]{1,0:T(8,128)S(1)}, u32[]{:S(2)}) copy-start(f32[1024,768]{1,0:T(8,128)S(1)} %get-tuple-element.609) | copy-start | bytes 9437188
  218.3 20.3 %copy-start.81 = (f32[1024]{0:T(1024)}, f32[1024]{0:T(1024)S(1)}, u32[]{:S(2)}) copy-start(f32[1024]{0:T(1024)S(1)} %fusion.208) | copy-start | bytes 12292
  220.5 18.1 %copy-start.43 = (bf16[1024,768]{1,0:T(8,128)(2,1)}, bf16[1024,768]{1,0:T(8,128)(2,1)S(1)}, u32[]{:S(2)}) copy-start(bf16[1024,768]{1,0:T(8,128)(2,1)S(1)} %add_convert_fusion.2) | copy-start | bytes 4718596
  220.5 18.1 %copy-start.28 = (bf16[1024,768]{1,0:T(8,128)(2,1)S(1)}, bf16[1024,768]{1,0:T(8,128)(2,1)}, u32[]{:S(2)}) copy-start(bf16[1024,768]{1,0:T(8,128)(2,1)} %param.25) | copy-start | bytes 4718596
  220.5 18.1 %copy-start.65 = (f32[1024]{0:T(1024)S(1)}, f32[1024]{0:T(1024)}, u32[]{:S(2)}) copy-start(f32[1024]{0:T(1024)} %copy-done.64) | copy-start | bytes 12292
  220.5 18.1 %copy-start.110 = (bf16[2,768,768]{2,1,0:T(8,128)(2,1)S(1)}, bf16[2,768,768]{2,1,0:T(8,128)(2,1)}, u32[]{:S(2)}) copy-start(bf16[2,768,768]{2,1,0:T(8,128)(2,1)} %param.22) | copy-start | bytes 7077892
  244.9 145.7 %all-reduce.20.cloned.1.call-start = ((), (), s32[]{:S(2)}) async-start(), calls=%async_computation.4 | async-start | bytes 3145728 | tf_op jit(solution)/shard_map/psum | solution.py:134
  287.9 3.4 copy-start.72
  288.0 3.4 copy-start.80
  288.0 3.4 copy-start.82
  343.9 3.5 copy-start.48
  347.5 101.6 %all-reduce.22.cloned.1.call-start = ((), (), s32[]{:S(2)}) async-start(), calls=%async_computation.5 | async-start | bytes 3145728 | tf_op jit(solution)/shard_map/psum | solution.py:134
  347.7 4.5 copy-start.30
  347.7 4.5 copy-start.67
  347.7 4.5 copy-start.117
  352.2 38.3 %copy-start.4 = (f32[1024,768]{1,0:T(8,128)S(1)}, f32[1024,768]{1,0:T(8,128)}, u32[]{:S(2)}) copy-start(f32[1024,768]{1,0:T(8,128)} %copy-done.3) | copy-start | bytes 9437188
  352.2 38.3 %copy-start.70 = (f32[1024]{0:T(1024)S(1)}, f32[1024]{0:T(1024)}, u32[]{:S(2)}) copy-start(f32[1024]{0:T(1024)} %copy-done.69) | copy-start | bytes 12292
  352.2 38.3 %copy-start.78 = (f32[768]{0:T(1024)S(1)}, f32[768]{0:T(1024)}, u32[]{:S(2)}) copy-start(f32[768]{0:T(1024)} %copy-done.77) | copy-start | bytes 9220
  354.9 38.0 %copy-start.96 = (f32[1024]{0:T(1024)S(1)}, f32[1024]{0:T(1024)}, u32[]{:S(2)}) copy-start(f32[1024]{0:T(1024)} %copy-done.95) | copy-start | bytes 12292
  354.9 38.0 %copy-start.86 = (f32[1024]{0:T(1024)S(1)}, f32[1024]{0:T(1024)}, u32[]{:S(2)}) copy-start(f32[1024]{0:T(1024)} %copy-done.85) | copy-start | bytes 12292
  395.4 4.7 copy-start.116
  397.3 4.9 copy-start.25
  406.0 181.4 %all-reduce.26.cloned.1.call-start = ((), (), s32[]{:S(2)}) async-start(), calls=%async_computation.7 | async-start | bytes 6291456 | tf_op jit(solution)/shard_map/psum | solution.py:134
  406.1 3.8 copy-start.26
  406.1 3.8 copy-start.122
  409.8 39.2 %copy-start.1 = (bf16[1024,768]{1,0:T(8,128)(2,1)S(1)}, bf16[1024,768]{1,0:T(8,128)(2,1)}, u32[]{:S(2)}) copy-start(bf16[1024,768]{1,0:T(8,128)(2,1)} %param.17) | copy-start | bytes 4718596
  409.8 39.2 %copy-start.8 = (bf16[1024,768]{1,0:T(8,128)(2,1)S(1)}, bf16[1024,768]{1,0:T(8,128)(2,1)}, u32[]{:S(2)}) copy-start(bf16[1024,768]{1,0:T(8,128)(2,1)} %all-reduce.12.cloned.1.call-done) | copy-start | bytes 4718596
  409.8 39.2 %copy-start.61 = (f32[1024]{0:T(1024)S(1)}, f32[1024]{0:T(1024)}, u32[]{:S(2)}) copy-start(f32[1024]{0:T(1024)} %copy-done.60) | copy-start | bytes 12292
  409.9 39.2 %copy-start.63 = (f32[768]{0:T(1024)S(1)}, f32[768]{0:T(1024)}, u32[]{:S(2)}) copy-start(f32[768]{0:T(1024)} %copy-done.62) | copy-start | bytes 9220
  412.4 39.3 %copy-start.94 = (f32[1024]{0:T(1024)S(1)}, f32[1024]{0:T(1024)}, u32[]{:S(2)}) copy-start(f32[1024]{0:T(1024)} %copy-done.93) | copy-start | bytes 12292
  412.4 39.4 %copy-start.76 = (f32[1024]{0:T(1024)S(1)}, f32[1024]{0:T(1024)}, u32[]{:S(2)}) copy-start(f32[1024]{0:T(1024)} %copy-done.75) | copy-start | bytes 12292
  456.4 4.0 copy-start.6
  456.4 4.0 copy-start.13
  456.4 4.0 copy-start.59
  518.5 3.5 copy-start.42
  518.6 310.3 %all-reduce.24.cloned.1.call-start = ((), (), s32[]{:S(2)}) async-start(), calls=%async_computation.6 | async-start | bytes 14155776 | tf_op jit(solution)/shard_map/psum | solution.py:234
  530.8 4.0 copy-start.103
  533.1 58.4 %copy-start.92 = (f32[1024]{0:T(1024)S(1)}, f32[1024]{0:T(1024)}, u32[]{:S(2)}) copy-start(f32[1024]{0:T(1024)} %copy-done.91) | copy-start | bytes 12292
  587.4 4.1 copy-start.21
  589.2 44.9 %copy-start.68 = (f32[1024]{0:T(1024)S(1)}, f32[1024]{0:T(1024)}, u32[]{:S(2)}) copy-start(f32[1024]{0:T(1024)} %copy-done.64) | copy-start | bytes 12292
  634.1 4.3 copy-start.11
  828.9 5.9 copy-start.39
  (67 other events, 138.1 us)
Sparse Core Ops, SparseCore 0:
  39.2 45.5 all-reduce.11
  102.2 42.8 all-reduce.13
  172.0 42.8 all-reduce.15
  245.0 42.8 all-reduce.17
  347.6 42.8 all-reduce.19
  406.1 42.8 all-reduce.21
  518.7 68.6 all-reduce.25
  592.4 236.4 all-reduce.23
where the time goes:
time: 857 us; the launch traced here: 847 us
  waiting for transfers between devices  481 us (56%)
  matrix products  127 us (15%)
  other arithmetic  94.3 us (11%)
  local copies, waits for them, and re-layouts  66.2 us (8%)
  blocking collectives  39.3 us (5%)
  loops' own time  21.1 us (2%)
  between operations  16.8 us (2%)
    psum x7, waiting for transfers between devices, group_total(): lax.psum(partial_value.astype(jnp.bfloat16), 'tensor').astype(jnp.float32)  292 us
    psum x1, waiting for transfers between devices, per_device(): lax.psum(stacked[0].astype(jnp.bfloat16), 'dp').astype(jnp.float32)  188 us
    psum x1, blocking collectives, per_device(): lax.psum(stacked[4].astype(jnp.bfloat16), 'dp').astype(jnp.float32)  39.3 us
    dynamic_update_slice x8, local copies, waits for them, and re-layouts, attend_backward(): lax.scan(one_block, (zeros_acc, zeros_acc), jnp.arange(seq_count * per_se...  31.5 us
    dot_general x2, matrix products, per_device(): hidden = jnp.dot(normed_mid, proj_up, preferred_element_type=jnp.float32)  27.1 us
    reduce_sum x11, other arithmetic, norm_rows(): return centre * lax.rsqrt(spread + 1e-05) * gain_row + bias_row  23.6 us
  transfers between devices with their start and end apart: 8, of which 8 were waited for; matrix products, arithmetic and copies ran while one was open for 6% of the time, Pallas kernels for 0%

commit v1 on v0

--- a/solution.py
+++ b/solution.py
@@ -1,12 +1,250 @@
+import functools
+
 import jax
 import jax.numpy as jnp
 from jax import lax
+from jax.experimental import pallas as pl
+from jax.experimental.pallas import tpu as pltpu
 from jax.sharding import PartitionSpec as P
 
 HEAD_DIM = 64
+LANES = 128
+BF16 = jnp.bfloat16
+F32 = jnp.float32
+MESH = pl.DeviceIdType.MESH
+ANY = pl.BlockSpec(memory_space=pl.ANY)
+VMEM = pl.BlockSpec(memory_space=pltpu.VMEM)
+SMEM = pl.BlockSpec(memory_space=pltpu.SMEM)
+
+
+def dot_nn(a, b):
+    return lax.dot_general(a, b, (((1,), (0,)), ((), ())), preferred_element_type=F32)
+
+
+def dot_nt(a, b):
+    return lax.dot_general(a, b, (((1,), (1,)), ((), ())), preferred_element_type=F32)
+
+
+def dot_tn(a, b):
+    return lax.dot_general(a, b, (((0,), (0,)), ((), ())), preferred_element_type=F32)
 
 
 def norm_rows(values_in, gain_row, bias_row):
+    centre = values_in - jnp.mean(values_in, axis=-1, keepdims=True)
+    spread = jnp.mean(centre * centre, axis=-1, keepdims=True)
+    return centre * lax.rsqrt(spread + 1e-05) * gain_row + bias_row
+
+
+def gelu_pair(u):
+    bell = jnp.exp(u * u * -0.5)
+    t = 1.0 / (1.0 + 0.23164189 * jnp.abs(u))
+    series = t * (0.127414796 + t * (-0.142248368 + t * (0.7107068705 + t * (-0.7265760135 + t * 0.5307027145))))
+    tail = series * bell
+    phi_cdf = jnp.where(u >= 0.0, 1.0 - tail, tail)
+    return u * phi_cdf, phi_cdf + u * bell * 0.3989422804014327
+
+
+class Chunks:
+    def __init__(self, rows, count):
+        self.rows, self.count = rows, count
+        self.half = rows // 2
+
+    def all(self, c):
+        return pl.ds(c * self.rows, self.rows)
+
+    def part(self, c, b):
+        return pl.ds(pl.multiple_of(c * self.rows + b * self.half, self.half), self.half)
+
+
+def forward_kernel(n_tensor, len_ref, x_hbm, wqkv_hbm, wout_hbm, wup_hbm, wdown_hbm, gain_ref, bias_ref, act_out,
+                   xin, wqkv, wout, wup, wdown, normed, nmid, q_s, k_s, kt_s, v_s, ctx, lse, xh, midh, act, gpr,
+                   part, rsbuf, ysend, yrecv, result, sems_in, rs_sem, y_sem, ag_sem, out_sem):
+    layers = wqkv.shape[0]
+    rows_all, width = xin.shape
+    ch = Chunks(256, rows_all // 256)
+    C = ch.count
+    dp, t = lax.axis_index("dp"), lax.axis_index("tensor")
+    b = lax.rem(t, 2)
+    sib = (dp, t + 1 - 2 * b)
+    peer = (dp, lax.rem(t + 2, n_tensor))
+    length = len_ref[0]
+
+    loads = [(x_hbm, xin), (wqkv_hbm, wqkv), (wout_hbm, wout), (wup_hbm, wup), (wdown_hbm, wdown)]
+    loads = [pltpu.make_async_copy(a, o, sems_in.at[i]) for i, (a, o) in enumerate(loads)]
+    for cp in loads:
+        cp.start()
+    waited = set()
+
+    def need(i):
+        if i not in waited:
+            waited.add(i)
+            loads[i].wait()
+
+    barrier = pltpu.get_barrier_semaphore()
+    for other in (sib, peer):
+        pl.semaphore_signal(barrier, inc=1, device_id=other, device_id_type=MESH)
+    pl.semaphore_wait(barrier, 2)
+
+    def remote(src, dst, sem, dev):
+        return pltpu.make_async_remote_copy(src_ref=src, dst_ref=dst, send_sem=sem.at[0], recv_sem=sem.at[1],
+                                            device_id=dev, device_id_type=MESH)
+
+    mine, others = pl.ds(pl.multiple_of(b * ch.half, ch.half), ch.half), pl.ds(pl.multiple_of((1 - b) * ch.half, ch.half), ch.half)
+
+    def rs_copy(p, c):
+        s = p % 2
+        return remote(part.at[s, c, others], rsbuf.at[s, c], rs_sem.at[s, c], sib)
+
+    def y_copy(p, c):
+        s = p % 2
+        return remote(ysend.at[s, c], yrecv.at[s, c], y_sem.at[s, c], peer)
+
+    def ag_copy(p, c):
+        buf = {0: nmid.at[0], 1: normed.at[1], 2: nmid.at[1], 3: result}[p]
+        rows = ch.part(c, b)
+        return remote(buf.at[rows], buf.at[rows], ag_sem.at[p % 2, c], sib)
+
+    gain = lambda l, i: gain_ref[pl.ds(2 * l + i, 1), :]
+    bias = lambda l, i: bias_ref[pl.ds(2 * l + i, 1), :]
+    lane = lax.broadcasted_iota(jnp.int32, (ch.rows, LANES), 1)
+    low = lane < HEAD_DIM
+
+    def attend(l, c):
+        need(1)
+        rows = ch.all(c)
+        if l == 0:
+            need(0)
+            normed[0, rows] = norm_rows(xin[rows].astype(F32), gain(0, 0), bias(0, 0)).astype(BF16)
+        nc = normed[l, rows]
+        q = dot_nn(nc, wqkv[l, 0]).astype(BF16) * jnp.asarray(HEAD_DIM ** (-0.5), BF16)
+        k = dot_nn(nc, wqkv[l, 1])
+        q_s[l, rows] = q
+        k_s[l, rows] = k.astype(BF16)
+        kt_s[l, :, rows] = k.T.astype(BF16)
+        v_s[l, rows] = dot_nn(nc, wqkv[l, 2]).astype(BF16)
+        wide = (c + 1) * ch.rows
+        key_pos = lax.broadcasted_iota(jnp.int32, (ch.rows, wide), 1)
+        query_pos = lax.broadcasted_iota(jnp.int32, (ch.rows, wide), 0) + c * ch.rows
+        allowed = (key_pos <= query_pos) & (key_pos < length)
+        outs = []
+        logs = jnp.zeros((ch.rows, LANES), F32)
+        for h in range(3):
+            lanes = slice(0, LANES) if h < 2 else slice(LANES, 2 * LANES)
+            qh = q[:, lanes]
+            if h == 0:
+                qh = jnp.where(low, qh, jnp.zeros_like(qh))
+            elif h == 1:
+                qh = jnp.where(low, jnp.zeros_like(qh), qh)
+            s = dot_nt(qh, k_s[l, 0:wide, lanes])
+            s = jnp.where(allowed, s, -1e30)
+            m = jnp.max(s, axis=-1, keepdims=True)
+            p = jnp.exp(s - m)
+            z = jnp.sum(p, axis=-1, keepdims=True)
+            outs.append(dot_nn(p.astype(BF16), v_s[l, 0:wide, lanes]) / z)
+            logs = jnp.where(lane == h, m + jnp.log(z), logs)
+        lse[l, :, rows] = logs.T[0:8, :]
+        ctx[l, rows, 0:LANES] = jnp.where(low, outs[0], outs[1]).astype(BF16)
+        ctx[l, rows, LANES:2 * LANES] = outs[2].astype(BF16)
+        need(2)
+        part[0, c] = dot_nn(ctx[l, rows], wout[l]).astype(BF16)
+
+    def feed(l, c):
+        need(3)
+        rows = ch.all(c)
+        nm = nmid[l, rows]
+        ff = wup.shape[2]
+        for n in range(0, ff, 256):
+            u = dot_nn(nm, wup[l, :, n:n + 256])
+            a, g = gelu_pair(u)
+            act[l, rows, n:n + 256] = a.astype(BF16)
+            gpr[l, rows, n:n + 256] = g.astype(BF16)
+        need(4)
+        part[1, c] = dot_nn(act[l, rows], wdown[l]).astype(BF16)
+
+    def compute(p, c):
+        (attend if p % 2 == 0 else feed)(p // 2, c)
+
+    def sum_pair(p, c):
+        s = p % 2
+        rs_copy(p, c).wait()
+        ysend[s, c] = (part[s, c, mine, :].astype(F32) + rsbuf[s, c].astype(F32)).astype(BF16)
+        y_copy(p, c).start()
+
+    def finish(p, c):
+        s, l = p % 2, p // 2
+        y_copy(p, c).wait()
+        rows = ch.part(c, b)
+        total = ysend[s, c].astype(F32) + yrecv[s, c].astype(F32)
+        if s == 0:
+            before = xin[rows].astype(F32) if l == 0 else xh[c]
+            middle = before + total
+            midh[l, c] = middle
+            nmid[l, rows] = norm_rows(middle, gain(l, 1), bias(l, 1)).astype(BF16)
+        else:
+            pos = lax.broadcasted_iota(jnp.int32, (ch.half, width), 0) + c * ch.rows + b * ch.half
+            after = jnp.where(pos < length, midh[l, c] + total, 0.0)
+            if l + 1 < layers:
+                xh[c] = after
+                normed[l + 1, rows] = norm_rows(after, gain(l + 1, 0), bias(l + 1, 0)).astype(BF16)
+            else:
+                result[rows] = after.astype(BF16)
+        ag_copy(p, c).start()
+
+    steps = [(p, c) for p in range(2 * layers) for c in range(C)]
+    lag = C - 1
+    for i, (p, c) in enumerate(steps):
+        if p > 0:
+            ag_copy(p - 1, c).wait()
+        compute(p, c)
+        rs_copy(p, c).start()
+        if i >= lag:
+            finish(*steps[i - lag])
+        sum_pair(p, c)
+    for i in range(len(steps) - lag, len(steps)):
+        finish(*steps[i])
+    for c in range(C):
+        ag_copy(2 * layers - 1, c).wait()
+    out = pltpu.make_async_copy(result, act_out, out_sem.at[0])
+    out.start()
+    out.wait()
+
+
+def forward_call(mesh, lengths, x, wqkv, wout, wup, wdown, gain, bias):
+    rows, width = x.shape
+    layers, ff = wup.shape[0], wup.shape[2]
+    C = rows // 256
+    half = (C, 128, width)
+    scratch = [
+        pltpu.VMEM(x.shape, BF16), pltpu.VMEM(wqkv.shape, BF16), pltpu.VMEM(wout.shape, BF16),
+        pltpu.VMEM(wup.shape, BF16), pltpu.VMEM(wdown.shape, BF16),
+        pltpu.VMEM((layers, rows, width), BF16), pltpu.VMEM((layers, rows, width), BF16),
+        pltpu.VMEM((layers, rows, 256), BF16), pltpu.VMEM((layers, rows, 256), BF16),
+        pltpu.VMEM((layers, 256, rows), BF16), pltpu.VMEM((layers, rows, 256), BF16),
+        pltpu.VMEM((layers, rows, 256), BF16), pltpu.VMEM((layers, 8, rows), F32),
+        pltpu.VMEM(half, F32), pltpu.VMEM((layers,) + half, F32),
+        pltpu.VMEM((layers, rows, ff), BF16), pltpu.VMEM((layers, rows, ff), BF16),
+        pltpu.VMEM((2, C, 256, width), BF16), pltpu.VMEM((2,) + half, BF16), pltpu.VMEM((2,) + half, BF16),
+        pltpu.VMEM((2,) + half, BF16), pltpu.VMEM((rows, width), BF16),
+        pltpu.SemaphoreType.DMA((5,)), pltpu.SemaphoreType.DMA((2, C, 2)), pltpu.SemaphoreType.DMA((2, C, 2)),
+        pltpu.SemaphoreType.DMA((2, C, 2)), pltpu.SemaphoreType.DMA((1,)),
+    ]
+    return pl.pallas_call(
+        functools.partial(forward_kernel, mesh.shape["tensor"]),
+        out_shape=jax.ShapeDtypeStruct((rows, width), BF16),
+        in_specs=[SMEM, ANY, ANY, ANY, ANY, ANY, VMEM, VMEM], out_specs=ANY, scratch_shapes=scratch,
+        compiler_params=pltpu.CompilerParams(collective_id=0, has_side_effects=True, vmem_limit_bytes=60 * 2**20),
+        name="forward",
+    )(lengths, x, wqkv, wout, wup, wdown, gain, bias)
+
+
+def pad_weights(qkv_weight, out_weight):
+    layers, width, three, part_width = qkv_weight.shape
+    wqkv = jnp.pad(jnp.swapaxes(qkv_weight, 1, 2), ((0, 0), (0, 0), (0, 0), (0, 256 - part_width)))
+    wout = jnp.pad(out_weight, ((0, 0), (0, 256 - part_width), (0, 0)))
+    return wqkv, wout
+
+
+def norm_rows_full(values_in, gain_row, bias_row):
     centre = values_in - jnp.mean(values_in, axis=-1, keepdims=True)
     spread = jnp.mean(centre * centre, axis=-1, keepdims=True)
     return centre * lax.rsqrt(spread + 1e-05) * gain_row + bias_row
@@ -118,7 +356,7 @@
 
 
 def per_device(
-    inputs, lengths, qkv_weight, out_weight, up_weight, down_weight, norm_gain, norm_bias, cotangent
+    mesh, inputs, lengths, qkv_weight, out_weight, up_weight, down_weight, norm_gain, norm_bias, cotangent
 ):
     layer_total = qkv_weight.shape[0]
     row_total, width_all = inputs.shape
@@ -147,7 +385,7 @@
     stored = []
     for layer_id in range(layer_total):
         proj_qkv, proj_out, proj_up, proj_down, gain_rows, biases = layer_weights(layer_id)
-        normed = norm_rows(stream, gain_rows[0], biases[0]).astype(jnp.bfloat16)
+        normed = norm_rows_full(stream, gain_rows[0], biases[0]).astype(jnp.bfloat16)
         projected = jnp.dot(normed, proj_qkv, preferred_element_type=jnp.float32).astype(
             jnp.bfloat16
         )
@@ -157,7 +395,7 @@
         middle = stream + group_total(
             jnp.dot(context, proj_out, preferred_element_type=jnp.float32)
         )
-        normed_mid = norm_rows(middle, gain_rows[1], biases[1]).astype(jnp.bfloat16)
+        normed_mid = norm_rows_full(middle, gain_rows[1], biases[1]).astype(jnp.bfloat16)
         hidden = jnp.dot(normed_mid, proj_up, preferred_element_type=jnp.float32)
         activated = exact_gelu(hidden).astype(jnp.bfloat16)
         stored.append(
@@ -166,7 +404,8 @@
         stream = valid_rows * (
             middle + group_total(jnp.dot(activated, proj_down, preferred_element_type=jnp.float32))
         )
-    outputs = stream.astype(jnp.bfloat16)
+    wqkv, wout = pad_weights(qkv_weight, out_weight)
+    outputs = forward_call(mesh, lengths, inputs, wqkv, wout, up_weight, down_weight, norm_gain.reshape(-1, width_all), norm_bias.reshape(-1, width_all))
     upstream = cotangent.astype(jnp.float32)
     grad_layers = []
     for layer_id in reversed(range(layer_total)):
@@ -192,7 +431,7 @@
         mid_norm_grad = group_total(
             jnp.einsum("tf,df->td", hidden_grad, proj_up, preferred_element_type=jnp.float32)
         )
-        unused_mid, norm_pull = jax.vjp(norm_rows, middle, gain_rows[1], biases[1])
+        unused_mid, norm_pull = jax.vjp(norm_rows_full, middle, gain_rows[1], biases[1])
         middle_grad, gain_mid, bias_mid = norm_pull(mid_norm_grad)
         upstream = upstream + middle_grad
         out_grad = upstream.astype(jnp.bfloat16)
@@ -215,7 +454,7 @@
         in_norm_grad = group_total(
             jnp.einsum("tc,dc->td", proj_grad, proj_qkv, preferred_element_type=jnp.float32)
         )
-        unused_in, norm_pull = jax.vjp(norm_rows, stream_in, gain_rows[0], biases[0])
+        unused_in, norm_pull = jax.vjp(norm_rows_full, stream_in, gain_rows[0], biases[0])
         stream_grad, gain_in, bias_in = norm_pull(in_norm_grad)
         upstream = upstream + stream_grad
         grad_layers.append(
@@ -264,5 +503,5 @@
         P(),
     )
     return jax.shard_map(
-        per_device, mesh=mesh, in_specs=in_specs, out_specs=out_specs, check_vma=False
+        functools.partial(per_device, mesh), mesh=mesh, in_specs=in_specs, out_specs=out_specs, check_vma=False
     )

time: 857 us -> 868 us (1.013)
  waiting for transfers between devices: 481 us -> 374 us
  Pallas kernels: 0 us -> 90.2 us
  matrix products: 127 us -> 143 us
  local copies, waits for them, and re-layouts: 66.2 us -> 80.7 us
    pallas_call x0 -> x1, Pallas kernels: none -> 90.2 us  [forward_call(): pl.pallas_call(functools.partial(forward_kernel, mesh.shape['tensor']), o...]
    psum x7, waiting for transfers between devices: 292 us -> 236 us  [group_total(): lax.psum(partial_value.astype(jnp.bfloat16), 'tensor').astype(jnp.float32)]
    psum x1, waiting for transfers between devices: 188 us -> 139 us  [per_device(): lax.psum(stacked[0].astype(jnp.bfloat16), 'dp').astype(jnp.float32)]
    unnamed x248 -> x242, local copies, waits for them, and re-layouts: 16.8 us -> 19.7 us
  transfers between devices with their start and end apart: 8 -> 8, of which waited for: 8 -> 7; matrix products, arithmetic and copies ran while one was open for 6% -> 6% of each run, Pallas kernels for 0% -> 11%
where the time goes in v1:
time: 868 us; the launch traced here: 858 us
  waiting for transfers between devices  374 us (43%)
  matrix products  143 us (16%)
  other arithmetic  91.3 us (11%)
  Pallas kernels  90.2 us (10%)
  local copies, waits for them, and re-layouts  80.7 us (9%)
  blocking collectives  39.5 us (5%)
  loops' own time  20.6 us (2%)
  between operations  16.8 us (2%)
    psum x7, waiting for transfers between devices, group_total(): lax.psum(partial_value.astype(jnp.bfloat16), 'tensor').astype(jnp.float32)  236 us
    psum x1, waiting for transfers between devices, per_device(): lax.psum(stacked[0].astype(jnp.bfloat16), 'dp').astype(jnp.float32)  139 us
    pallas_call x1, Pallas kernels, forward_call(): pl.pallas_call(functools.partial(forward_kernel, mesh.shape['tensor']), o...  90.2 us
    psum x1, blocking collectives, per_device(): lax.psum(stacked[4].astype(jnp.bfloat16), 'dp').astype(jnp.float32)  39.5 us
    dynamic_update_slice x8, local copies, waits for them, and re-layouts, attend_backward(): lax.scan(one_block, (zeros_acc, zeros_acc), jnp.arange(seq_count * per_se...  33 us
    dot_general x2, matrix products, per_device(): hidden = jnp.dot(normed_mid, proj_up, preferred_element_type=jnp.float32)  25.6 us
    reduce_sum x11, other arithmetic, norm_rows_full(): return centre * lax.rsqrt(spread + 1e-05) * gain_row + bias_row  24.9 us
    unnamed x242, local copies, waits for them, and re-layouts  19.7 us
  transfers between devices with their start and end apart: 8, of which 7 were waited for; matrix products, arithmetic and copies ran while one was open for 6% of the time, Pallas kernels for 11%

profile of v1, /device:TPU:0, one launch (start us, length us, event | category | flops | bytes accessed | tf_op | source)
XLA Modules:
  0.0 858.1 jit_solution(11807382393775321359)
XLA Ops:
  9.1 2.0 fusion.125
  15.8 20.1 %while.60 = (s32[]{:T(128)}, bf16[2,512,3,64]{1,3,2,0:T(8,128)(2,1)S(1)}, f32[2,3,512]{2,1,0:T(4,128)S(1)}, s32[2]{0:T(128)S(1)}, s32[1]{0:T(128)}, /*index=5*/b...) while((s32[]{:T(128)}, ...), condition=%wide.region_5.6_spmd, body=%wide.region_2.5_spmd.sunk | while | flops 422674432 | bytes 22217024 | solution.py:299
  22.7 3.2 fusion.288
  32.7 3.2 fusion.288
  39.3 45.4 %all-reduce.13.cloned.1.call-done = bf16[1024,768]{1,0:T(8,128)(2,1)} async-done(((bf16[1024,768]{1,0:T(8,128)(2,1)}), bf16[1024,768]{1,0:T(8,128)(2,1)}) %all-reduce.13.cloned.1.call-update) | async-done | bytes 1572880 | tf_op jit(solution)/shard_map/psum | solution.py:372
  84.8 2.0 fusion.141
  89.2 9.0 %multiply_convert_fusion.3 = (bf16[1024,768]{1,0:T(8,128)(2,1)S(1)}, f32[1024,768]{1,0:T(8,128)}, f32[1024,768]{1,0:T(8,128)}) fusion(bf16[1024,768]{1,0:T(8,128)(2,1)S(1)} %add_convert_fusion.4, bf16[2,768,768]{2,1,0:T(8,128)(2,1)S(1)} %copy-done.46), kind=kOutput, calls=%fused_computation.189 | convolution fusion | flops 1259077632 | bytes 10616832 | tf_op jit(solution)/shard_map/dot_general | solution.py:399
  99.4 2.5 convolution_convert_fusion.5
  103.0 42.1 %all-reduce.15.cloned.1.call-done = bf16[1024,768]{1,0:T(8,128)(2,1)} async-done(((bf16[1024,768]{1,0:T(8,128)(2,1)}), bf16[1024,768]{1,0:T(8,128)(2,1)}) %all-reduce.15.cloned.1.call-update) | async-done | bytes 1572880 | tf_op jit(solution)/shard_map/psum | solution.py:372
  145.1 2.2 fusion.217
  152.3 23.2 %while.61 = (s32[]{:T(128)}, bf16[2,512,3,64]{1,3,2,0:T(8,128)(2,1)}, f32[2,3,512]{2,1,0:T(4,128)S(1)}, s32[2]{0:T(128)S(1)}, s32[1]{0:T(128)}, /*index=5*/bf16[...) while((s32[]{:T(128)}, ...), condition=%wide.region_15.16_spmd, body=%wide.region_12.15_spmd.sunk | while | flops 422674432 | bytes 22212928 | solution.py:299
  155.9 2.3 fusion.291
  160.0 3.8 fusion.293
  167.5 2.3 fusion.291
  171.7 3.8 fusion.293
  177.9 2.7 convolution_convert_fusion.4
  181.2 42.5 %all-reduce.17.cloned.1.call-done = bf16[1024,768]{1,0:T(8,128)(2,1)} async-done(((bf16[1024,768]{1,0:T(8,128)(2,1)}), bf16[1024,768]{1,0:T(8,128)(2,1)}) %all-reduce.17.cloned.1.call-update) | async-done | bytes 1572880 | tf_op jit(solution)/shard_map/psum | solution.py:372
  228.3 16.6 %fusion.128 = (f32[1024,768]{1,0:T(8,128)S(1)}, f32[1024,768]{1,0:T(8,128)S(1)}) fusion(bf16[1024,768]{1,0:T(8,128)(2,1)S(1)} %add_convert_fusion.2, bf16[2,768,768]{2,1,0:T(8,128)(2,1)S(1)} %copy-done.47), kind=kOutput, calls=%fused_computation.163 | convolution fusion | flops 1256718336 | bytes 9043968 | tf_op jit(solution)/shard_map/dot_general | solution.py:418
  245.0 2.3 add_convert_fusion.1
  248.7 2.6 convolution_convert_fusion.3
  251.4 5.9 fusion.160
  257.3 37.1 %all-reduce.19.cloned.1.call-done = bf16[1024,768]{1,0:T(8,128)(2,1)} async-done(((bf16[1024,768]{1,0:T(8,128)(2,1)}), bf16[1024,768]{1,0:T(8,128)(2,1)}) %all-reduce.19.cloned.1.call-update) | async-done | bytes 1572880 | tf_op jit(solution)/shard_map/psum | solution.py:372
  294.4 4.3 fusion.121
  307.0 57.5 %while.62 = (s32[]{:T(128)}, f32[1,1024,3,64]{1,3,2,0:T(8,128)}, f32[1,1024,3,64]{1,3,2,0:T(8,128)}, bf16[2,512,3,64]{1,0,3,2:T(2,128)(2,1)}, s32[2]{0:T(128)}, ...) while((s32[]{:T(128)}, f32[1,1024,3,64]{1,3,2,0:T(8,128)}, ...), condition=%wide.region_24.25_spmd, body=%wide.region_22.24_spmd.sunk | while | flops 1032060928 | bytes 63295952 | solution.py:352
  312.1 2.0 fusion.302
  314.1 3.9 fusion.305
  318.0 3.5 multiply_reduce_fusion.7
  328.1 7.6 dynamic_update_slice.58
  340.8 2.0 fusion.302
  342.9 3.9 fusion.305
  346.8 3.5 multiply_reduce_fusion.7
  356.8 7.6 dynamic_update_slice.58
  368.4 2.6 convolution_convert_fusion.1
  371.4 4.5 fusion.158
  377.1 2.4 fusion.161
  379.5 34.6 %all-reduce.21.cloned.1.call-done = bf16[1024,768]{1,0:T(8,128)(2,1)} async-done(((bf16[1024,768]{1,0:T(8,128)(2,1)}), bf16[1024,768]{1,0:T(8,128)(2,1)}) %all-reduce.21.cloned.1.call-update) | async-done | bytes 1572880 | tf_op jit(solution)/shard_map/psum | solution.py:372
  414.1 2.3 fusion.119
  416.4 2.5 fusion.122
  421.6 2.1 copy-done.119
  423.6 2.2 add_convert_fusion
  425.8 2.6 convolution_convert_fusion.2
  428.5 3.9 fusion.159
  437.6 33.9 %all-reduce.23.cloned.1.call-done = bf16[1024,768]{1,0:T(8,128)(2,1)} async-done(((bf16[1024,768]{1,0:T(8,128)(2,1)}), bf16[1024,768]{1,0:T(8,128)(2,1)}) %all-reduce.23.cloned.1.call-update) | async-done | bytes 1572880 | tf_op jit(solution)/shard_map/psum | solution.py:372
  471.5 2.6 fusion.118
  474.2 3.3 fusion.123
  483.0 51.8 %while.63 = (s32[]{:T(128)}, f32[1,1024,3,64]{1,3,2,0:T(8,128)S(1)}, f32[1,1024,3,64]{1,3,2,0:T(8,128)}, bf16[2,512,3,64]{1,0,3,2:T(2,128)(2,1)}, s32[2]{0:T(128...) while((s32[]{:T(128)}, ...), condition=%wide.region_33.34_spmd, body=%wide.region_31.33_spmd.sunk | while | flops 1032060928 | bytes 55427452 | solution.py:352
  489.7 4.0 fusion.318
  493.7 3.6 multiply_reduce_fusion.8
  501.3 7.6 dynamic_update_slice.59
  515.5 4.0 fusion.318
  519.5 3.6 multiply_reduce_fusion.8
  527.1 7.6 dynamic_update_slice.59
  538.6 2.6 convolution_convert_fusion
  541.3 2.5 fusion.183
  549.4 2.7 copy.18
  554.9 90.2 %forward.1 = bf16[1024,768]{1,0:T(8,128)(2,1)} custom-call(s32[1]{0:T(128)} %copy.119.len_ref, bf16[1024,768]{1,0:T(8,128)(2,1)} %x_hbm.1, bf16[2,3,768,256]{3,2,1,0:T(8,128)(2,1)} %pad.8.wqkv_hbm, bf16[2,256,768]{2,1,0:T(8,128)(2,1)} %pad.9.wout_hbm, bf16[2,768,768]{2,1,0:T(8,128)(2,1)} %wup_hbm.1, bf16[2,768,768]{2,1,0:T(8,128)(2,1)} %wdown_hbm.1, ...), custom_call_target="tpu_custom_call" | custom-call | tf_op jit(solution)/shard_map/forward/pallas_call | solution.py:231
  651.0 2.3 fusion.126
  655.4 39.5 %all-reduce.2 = (bf16[2,2,768]{2,1,0:T(2,128)(2,1)S(1)}, bf16[2,2,768]{2,1,0:T(2,128)(2,1)S(1)}) all-reduce(bf16[2,2,768]{2,1,0:T(2,128)(2,1)S(1)} %pad_maximum_fusion.4, bf16[2,2,768]{2,1,0:T(2,128)(2,1)S(1)} %pad_maximum_fusion.5), channel_id=1, replica_groups=mesh['dp'=8,'tensor'=4] {'dp'}, use_global_device_ids=true, to_apply=%region_45.46 | all-reduce | flops 6144 | bytes 24576 | tf_op jit(solution)/shard_map/psum | solution.py:477
  696.1 3.8 add_add_fusion.4
  699.9 138.7 %all-reduce.27.cloned.1.call-done = (bf16[2,768,3,192]{1,3,2,0:T(8,128)(2,1)}, bf16[2,192,768]{2,1,0:T(8,128)(2,1)}, bf16[2,768,768]{2,1,0:T(8,128)(2,1)}, bf16[2,768,768]{2,1,0:T(8,128)(2,1)}) async-done(((bf16[2,768,3,192]{1,3,2,0:T(8,128)(2,1)}, bf16[2,192,768]{2,1,0:T(8,128)(2,1)}, bf16[2,768,768]{2,1,0:T(8,128)(2,1)}, bf16[2,768,768]{2,1,0:T(8,128)(2,1)}), (bf16[2,768,3,192]{1,3,2,0:T(8,128)(2,1)}, ...) | async-done | bytes 7077904 | tf_op jit(solution)/shard_map/psum | solution.py:473
  838.6 2.3 convert_element_type.269
  841.0 3.6 convert_element_type.268
  844.5 2.5 convert_element_type.270
  847.1 2.5 convert_element_type.272
  (422 shorter events, 125.7 us)
Async XLA Ops:
  7.2 4.6 copy-start.28
  7.2 77.6 %all-reduce.13.cloned.1.call-start = ((), (), s32[]{:S(2)}) async-start(), calls=%async_computation | async-start | bytes 3145728 | tf_op jit(solution)/shard_map/psum | solution.py:372
  7.2 5.6 copy-start.92
  7.2 5.5 copy-start.94
  7.2 6.3 copy-start
  9.1 5.8 copy-start.80
  13.5 74.1 %copy-start.74 = (f32[768]{0:T(1024)}, f32[768]{0:T(1024)S(1)}, u32[]{:S(2)}) copy-start(f32[768]{0:T(1024)S(1)} %get-tuple-element.631) | copy-start | bytes 9220
  13.5 134.9 %copy-start.84 = (f32[768]{0:T(1024)}, f32[768]{0:T(1024)S(1)}, u32[]{:S(2)}) copy-start(f32[768]{0:T(1024)S(1)} %get-tuple-element.629) | copy-start | bytes 9220
  13.5 134.9 %copy-start.116 = (f32[768]{0:T(1024)}, f32[768]{0:T(1024)S(1)}, u32[]{:S(2)}) copy-start(f32[768]{0:T(1024)S(1)} %get-tuple-element.519) | copy-start | bytes 9220
  15.8 21.4 %copy-start.33 = (bf16[2,192,768]{2,1,0:T(8,128)(2,1)S(1)}, bf16[2,192,768]{2,1,0:T(8,128)(2,1)}, u32[]{:S(2)}) copy-start(bf16[2,192,768]{2,1,0:T(8,128)(2,1)} %param.20) | copy-start | bytes 1769476
  36.0 50.7 %copy-start.5 = (bf16[1,1024,3,64]{1,3,2,0:T(8,128)(2,1)}, bf16[1,1024,3,64]{1,3,2,0:T(8,128)(2,1)S(1)}, u32[]{:S(2)}) copy-start(bf16[1,1024,3,64]{1,3,2,0:T(8,128)(2,1)S(1)} %get-tuple-element.1086) | copy-start | bytes 1179652
  39.0 106.0 %all-reduce.15.cloned.1.call-start = ((), (), s32[]{:S(2)}) async-start(), calls=%async_computation.1 | async-start | bytes 3145728 | tf_op jit(solution)/shard_map/psum | solution.py:372
  87.5 10.7 %copy-start.104 = (f32[1024]{0:T(1024)}, f32[1024]{0:T(1024)S(1)}, u32[]{:S(2)}) copy-start(f32[1024]{0:T(1024)S(1)} %multiply_reduce_fusion.4) | copy-start | bytes 12292
  87.6 10.7 %copy-start.82 = (f32[1024]{0:T(1024)}, f32[1024]{0:T(1024)S(1)}, u32[]{:S(2)}) copy-start(f32[1024]{0:T(1024)S(1)} %fusion.207) | copy-start | bytes 12292
  89.2 9.0 %copy-start.52 = (bf16[1024,768]{1,0:T(8,128)(2,1)}, bf16[1024,768]{1,0:T(8,128)(2,1)S(1)}, u32[]{:S(2)}) copy-start(bf16[1024,768]{1,0:T(8,128)(2,1)S(1)} %add_convert_fusion.4) | copy-start | bytes 4718596
  89.2 10.2 %copy-start.49 = (bf16[2,768,768]{2,1,0:T(8,128)(2,1)S(1)}, bf16[2,768,768]{2,1,0:T(8,128)(2,1)}, u32[]{:S(2)}) copy-start(bf16[2,768,768]{2,1,0:T(8,128)(2,1)} %wdown_hbm.1) | copy-start | bytes 7077892
  102.0 121.7 %all-reduce.17.cloned.1.call-start = ((), (), s32[]{:S(2)}) async-start(), calls=%async_computation.2 | async-start | bytes 3145728 | tf_op jit(solution)/shard_map/psum | solution.py:372
  103.0 44.3 %copy-start.70 = (f32[1024]{0:T(1024)}, f32[1024]{0:T(1024)S(1)}, u32[]{:S(2)}) copy-start(f32[1024]{0:T(1024)S(1)} %fusion.205) | copy-start | bytes 12292
  175.5 48.2 %copy-start.4 = (f32[1024,768]{1,0:T(8,128)S(1)}, f32[1024,768]{1,0:T(8,128)}, u32[]{:S(2)}) copy-start(f32[1024,768]{1,0:T(8,128)} %copy-done.3) | copy-start | bytes 9437188
  180.7 113.7 %all-reduce.19.cloned.1.call-start = ((), (), s32[]{:S(2)}) async-start(), calls=%async_computation.3 | async-start | bytes 3145728 | tf_op jit(solution)/shard_map/psum | solution.py:372
  226.0 18.8 %copy-start.108 = (f32[1024]{0:T(1024)}, f32[1024]{0:T(1024)S(1)}, u32[]{:S(2)}) copy-start(f32[1024]{0:T(1024)S(1)} %multiply_reduce_fusion.2) | copy-start | bytes 12292
  226.1 18.8 %copy-start.88 = (f32[1024]{0:T(1024)}, f32[1024]{0:T(1024)S(1)}, u32[]{:S(2)}) copy-start(f32[1024]{0:T(1024)S(1)} %fusion.209) | copy-start | bytes 12292
  228.3 16.6 %copy-start.54 = (bf16[1024,768]{1,0:T(8,128)(2,1)}, bf16[1024,768]{1,0:T(8,128)(2,1)S(1)}, u32[]{:S(2)}) copy-start(bf16[1024,768]{1,0:T(8,128)(2,1)S(1)} %add_convert_fusion.2) | copy-start | bytes 4718596
  228.3 16.6 %copy-start.23 = (bf16[1024,768]{1,0:T(8,128)(2,1)S(1)}, bf16[1024,768]{1,0:T(8,128)(2,1)}, u32[]{:S(2)}) copy-start(bf16[1024,768]{1,0:T(8,128)(2,1)} %param.25) | copy-start | bytes 4718596
  228.3 16.6 %copy-start.50 = (bf16[2,768,768]{2,1,0:T(8,128)(2,1)S(1)}, bf16[2,768,768]{2,1,0:T(8,128)(2,1)}, u32[]{:S(2)}) copy-start(bf16[2,768,768]{2,1,0:T(8,128)(2,1)} %wdown_hbm.1) | copy-start | bytes 7077892
  228.3 16.6 %copy-start.71 = (f32[1024]{0:T(1024)S(1)}, f32[1024]{0:T(1024)}, u32[]{:S(2)}) copy-start(f32[1024]{0:T(1024)} %copy-done.70) | copy-start | bytes 12292
  251.3 162.8 %all-reduce.21.cloned.1.call-start = ((), (), s32[]{:S(2)}) async-start(), calls=%async_computation.4 | async-start | bytes 3145728 | tf_op jit(solution)/shard_map/psum | solution.py:372
  294.4 4.4 copy-start.109
  294.4 4.4 copy-start.8
  294.4 4.4 copy-start.22
  294.4 4.4 copy-start.79
  294.4 4.4 copy-start.87
  294.4 4.4 copy-start.89
  371.0 4.8 copy-start.40
  371.0 6.1 copy-start.77
  371.0 6.1 copy-start.85
  371.0 6.0 copy-start.97
  371.1 6.0 copy-start.117
  371.1 100.4 %all-reduce.23.cloned.1.call-start = ((), (), s32[]{:S(2)}) async-start(), calls=%async_computation.5 | async-start | bytes 3145728 | tf_op jit(solution)/shard_map/psum | solution.py:372
  371.3 4.5 copy-start.31
  371.3 5.8 copy-start.56
  379.5 36.8 %copy-start.107 = (f32[1024]{0:T(1024)S(1)}, f32[1024]{0:T(1024)}, u32[]{:S(2)}) copy-start(f32[1024]{0:T(1024)} %copy-done.106) | copy-start | bytes 12292
  419.0 4.7 copy-start.119
  420.9 4.9 copy-start.26
  428.4 4.0 copy-start.32
  428.4 220.7 %all-reduce.25.cloned.1.call-start = ((), (), s32[]{:S(2)}) async-start(), calls=%async_computation.6 | async-start | bytes 3145728 | tf_op jit(solution)/shard_map/psum | solution.py:372
  435.9 35.6 %copy-start.1 = (bf16[1024,768]{1,0:T(8,128)(2,1)S(1)}, bf16[1024,768]{1,0:T(8,128)(2,1)}, u32[]{:S(2)}) copy-start(bf16[1024,768]{1,0:T(8,128)(2,1)} %x_hbm.1) | copy-start | bytes 4718596
  435.9 35.6 %copy-start.10 = (bf16[1024,768]{1,0:T(8,128)(2,1)S(1)}, bf16[1024,768]{1,0:T(8,128)(2,1)}, u32[]{:S(2)}) copy-start(bf16[1024,768]{1,0:T(8,128)(2,1)} %all-reduce.13.cloned.1.call-done) | copy-start | bytes 4718596
  435.9 35.6 %copy-start.69 = (f32[1024]{0:T(1024)S(1)}, f32[1024]{0:T(1024)}, u32[]{:S(2)}) copy-start(f32[1024]{0:T(1024)} %copy-done.68) | copy-start | bytes 12292
  436.0 35.6 %copy-start.75 = (f32[768]{0:T(1024)S(1)}, f32[768]{0:T(1024)}, u32[]{:S(2)}) copy-start(f32[768]{0:T(1024)} %copy-done.74) | copy-start | bytes 9220
  437.6 36.5 %copy-start.105 = (f32[1024]{0:T(1024)S(1)}, f32[1024]{0:T(1024)}, u32[]{:S(2)}) copy-start(f32[1024]{0:T(1024)} %copy-done.104) | copy-start | bytes 12292
  437.6 36.6 %copy-start.83 = (f32[1024]{0:T(1024)S(1)}, f32[1024]{0:T(1024)}, u32[]{:S(2)}) copy-start(f32[1024]{0:T(1024)} %copy-done.82) | copy-start | bytes 12292
  479.0 4.0 copy-start.6
  479.1 4.0 copy-start.15
  479.1 4.0 copy-start.67
  541.2 297.4 %all-reduce.27.cloned.1.call-start = ((), (), s32[]{:S(2)}) async-start(), calls=%async_computation.7 | async-start | bytes 14155776 | tf_op jit(solution)/shard_map/psum | solution.py:473
  548.2 4.0 copy-start.36
  554.9 92.1 %copy-start.113 = (bf16[768]{0:T(1024)(128)(2,1)S(1)}, bf16[768]{0:T(1024)(128)(2,1)}, u32[]{:S(2)}) copy-start(bf16[768]{0:T(1024)(128)(2,1)} %get-tuple-element.508) | copy-start | bytes 4612
  554.9 92.1 %copy-start.19 = (bf16[1024,768]{1,0:T(8,128)(2,1)S(1)}, bf16[1024,768]{1,0:T(8,128)(2,1)}, u32[]{:S(2)}) copy-start(bf16[1024,768]{1,0:T(8,128)(2,1)} %all-reduce.21.cloned.1.call-done) | copy-start | bytes 4718596
  645.1 4.1 copy-start.112
  645.1 5.9 copy-start.2
  647.3 6.0 copy-start.103
  649.2 4.1 copy-start.21
  838.6 5.9 copy-start.45
  (69 other events, 138.9 us)
Sparse Core Ops, SparseCore 0:
  39.2 45.5 all-reduce.12
  102.1 42.8 all-reduce.14
  180.8 42.8 all-reduce.16
  251.4 42.8 all-reduce.18
  371.1 42.8 all-reduce.20
  428.6 42.8 all-reduce.22
  541.3 55.6 all-reduce.24
  602.0 236.5 all-reduce.26
